TPU v7x, 256 devices: a whole 4x4x8 slice. The times are simulated.
256 devices in a mesh: row: 32 (over y, z), col: 8 (over x, core).
Axes of the slice: x: 4, y: 4, z: 8, core: 2. Of those that a mesh axis runs over, the one named last changes fastest.
Arguments:
- features: bfloat16 [65536, 128], P(('row', 'col')), may hold values from -6 to 6
- tiles: bfloat16 [32, 8, 128, 128, 128], P('row', 'col'), may hold values from -6 to 6
- block_rows: int32 [32, 8, 128], P('row', 'col'), may hold values from 0 to 15
- block_cols: int32 [32, 8, 128], P('row', 'col'), may hold values from 0 to 63
- labels: int32 [65536], P(('row', 'col')), may hold values from 0 to 171
- train_mask: int32 [65536], P(('row', 'col')), may hold values 0 or 1
- self_first: bfloat16 [128, 256], replicated, may hold values from -0.5 to 0.5
- neigh_first: bfloat16 [128, 256], replicated, may hold values from -0.5 to 0.5
- bias_first: float32 [256], replicated, may hold values from -4 to 4
- self_second: bfloat16 [256, 172], replicated, may hold values from -0.375 to 0.375
- neigh_second: bfloat16 [256, 172], replicated, may hold values from -0.375 to 0.375
- bias_second: float32 [172], replicated, may hold values from -4 to 4
Outputs:
- grad_self_first: float32 [128, 256], replicated
- grad_neigh_first: float32 [128, 256], replicated
- grad_bias_first: float32 [256], replicated
- grad_self_second: float32 [256, 172], replicated
- grad_neigh_second: float32 [256, 172], replicated
- grad_bias_second: float32 [172], replicated
All inputs are finite; a program needn't handle non-finite values. No bound on the sum of `train_mask` on one device may be relied on, other than what follows from the above.
Results may differ from a plain program's by a relative error of at most 0.014.
The roundings to bfloat16 on the way count: a program that leaves them out, or rounds other values in their place, can miss the bound.
Values may be sent and summed in bfloat16 or wider, within the bound.
No kernel may reach another device: no remote copies, remote signals or barrier semaphores. Data moves between devices by JAX's collectives and lax.ppermute only.
A program may use at most 128 MiB of HBM per device.

v0:
```python
import math

import jax
import jax.numpy as jnp
from jax import lax
from jax.sharding import PartitionSpec as P


def tile_product(tile_set, index_in, index_out, source, count_out, flipped):
    tile_edge = tile_set.shape[-1]
    columns = source.shape[1]
    tile_count = tile_set.shape[0]
    group_size = math.gcd(tile_count, 32)
    src_blocks = source.reshape(-1, tile_edge, columns)
    formula = "tji,tjf->tif" if flipped else "tij,tjf->tif"
    targets = jnp.arange(count_out, dtype=jnp.int32)

    def add_group(totals, offset):
        tile_group = lax.dynamic_slice_in_dim(tile_set, offset, group_size, 0)
        take_index = lax.dynamic_slice_in_dim(index_in, offset, group_size, 0)
        place_index = lax.dynamic_slice_in_dim(index_out, offset, group_size, 0)
        picked = jnp.take(src_blocks, take_index, axis=0)
        product = jnp.einsum(formula, tile_group, picked, preferred_element_type=jnp.float32)
        selector = (place_index[None, :] == targets[:, None]).astype(jnp.float32)
        added = jnp.dot(
            selector,
            product.reshape(group_size, tile_edge * columns),
            precision=lax.Precision.HIGHEST,
        )
        return (totals + added, None)

    starting = jnp.zeros((count_out, tile_edge * columns), jnp.float32)
    offsets = jnp.arange(0, tile_count, group_size, dtype=jnp.int32)
    totals, _ = lax.scan(add_group, starting, offsets)
    return totals.reshape(count_out * tile_edge, columns)


def on_device(
    features,
    tiles,
    block_rows,
    block_cols,
    labels,
    train_mask,
    self_first,
    neigh_first,
    bias_first,
    self_second,
    neigh_second,
    bias_second,
):
    tile_edge = tiles.shape[-1]
    tile_set = tiles.reshape(-1, tile_edge, tile_edge)
    rows_here = block_rows.reshape(-1)
    cols_here = block_cols.reshape(-1)
    local_rows = features.shape[0]
    col_count = lax.axis_size("col")
    row_count = lax.axis_size("row")
    span_blocks = col_count * local_rows // tile_edge
    source_blocks = row_count * local_rows // tile_edge
    loss_scale = 1.0 / math.sqrt(local_rows * col_count * row_count)
    gathered = lax.all_gather(features, "row", axis=0, tiled=True)
    first_part = tile_product(tile_set, cols_here, rows_here, gathered, span_blocks, False)
    squares = jnp.sum(jnp.square(tile_set.astype(jnp.float32)), axis=-1)
    chooser = (rows_here[None, :] == jnp.arange(span_blocks, dtype=jnp.int32)[:, None]).astype(
        jnp.float32
    )
    degree_part = jnp.dot(chooser, squares, precision=lax.Precision.HIGHEST).reshape(-1)
    first_sum, degree = (
        lax.psum_scatter(first_part, "col", scatter_dimension=0, tiled=True),
        lax.psum_scatter(degree_part, "col", scatter_dimension=0, tiled=True),
    )
    inverse = lax.rsqrt(1.0 + degree)
    first_agg = (inverse[:, None] * first_sum).astype(jnp.bfloat16)
    pre_first = (
        jnp.dot(features, self_first, preferred_element_type=jnp.float32)
        + jnp.dot(first_agg, neigh_first, preferred_element_type=jnp.float32)
        + bias_first
    )
    hidden = jnp.maximum(pre_first, 0.0).astype(jnp.bfloat16)
    hidden_rows = lax.all_gather(hidden, "row", axis=0, tiled=True)
    second_part = tile_product(tile_set, cols_here, rows_here, hidden_rows, span_blocks, False)
    second_sum = lax.psum_scatter(second_part, "col", scatter_dimension=0, tiled=True)
    second_agg = (inverse[:, None] * second_sum).astype(jnp.bfloat16)
    logits = (
        jnp.dot(hidden, self_second, preferred_element_type=jnp.float32)
        + jnp.dot(second_agg, neigh_second, preferred_element_type=jnp.float32)
        + bias_second
    )
    probabilities = jax.nn.softmax(logits, axis=-1)
    onehot = (labels[:, None] == jnp.arange(logits.shape[1], dtype=jnp.int32)[None, :]).astype(
        jnp.float32
    )
    logit_grad = (
        (probabilities - onehot) * (train_mask.astype(jnp.float32) * loss_scale)[:, None]
    ).astype(jnp.bfloat16)
    projected = (
        inverse[:, None] * jnp.dot(logit_grad, neigh_second.T, preferred_element_type=jnp.float32)
    ).astype(jnp.bfloat16)
    span_grad = lax.all_gather(projected, "col", axis=0, tiled=True)
    backflow_part = tile_product(tile_set, rows_here, cols_here, span_grad, source_blocks, True)
    backflow = lax.psum_scatter(backflow_part, "row", scatter_dimension=0, tiled=True)
    hidden_grad = jnp.dot(logit_grad, self_second.T, preferred_element_type=jnp.float32) + backflow
    pre_grad = jnp.where(pre_first > 0, hidden_grad, 0.0).astype(jnp.bfloat16)
    local_grads = (
        jnp.einsum("vi,vj->ij", features, pre_grad, preferred_element_type=jnp.float32),
        jnp.einsum("vi,vj->ij", first_agg, pre_grad, preferred_element_type=jnp.float32),
        jnp.sum(pre_grad.astype(jnp.float32), axis=0),
        jnp.einsum("vi,vj->ij", hidden, logit_grad, preferred_element_type=jnp.float32),
        jnp.einsum("vi,vj->ij", second_agg, logit_grad, preferred_element_type=jnp.float32),
        jnp.sum(logit_grad.astype(jnp.float32), axis=0),
    )
    (
        grad_self_first,
        grad_neigh_first,
        grad_bias_first,
        grad_self_second,
        grad_neigh_second,
        grad_bias_second,
    ) = lax.psum(
        (
            local_grads[0],
            local_grads[1],
            local_grads[2],
            local_grads[3],
            local_grads[4],
            local_grads[5],
        ),
        ("row", "col"),
    )
    return (
        grad_self_first,
        grad_neigh_first,
        grad_bias_first,
        grad_self_second,
        grad_neigh_second,
        grad_bias_second,
    )


def solution(mesh):
    in_specs = (
        P(("row", "col"), None),
        P("row", "col", None, None, None),
        P("row", "col", None),
        P("row", "col", None),
        P(("row", "col")),
        P(("row", "col")),
        P(),
        P(),
        P(),
        P(),
        P(),
        P(),
    )
    out_specs = (P(), P(), P(), P(), P(), P())
    return jax.shard_map(
        on_device, mesh=mesh, in_specs=in_specs, out_specs=out_specs, check_vma=False
    )
```

profile of v0, /device:TPU:1, one launch (start us, length us, event | category | flops | bytes accessed | tf_op | source)
XLA Modules:
  0.0 957.6 jit_solution(13446118578903883237)
XLA Ops:
  8.0 80.5 %all-gather.4.cloned.1.call-done = bf16[8192,128]{1,0:T(8,128)(2,1)} async-done(((bf16[256,128]{1,0:T(8,128)(2,1)}), bf16[8192,128]{1,0:T(8,128)(2,1)}) %all-gather.4.cloned.1.call-update) | async-done | bytes 2097168 | tf_op jit(solution)/shard_map/all_gather | solution.py:62
  88.5 42.2 %while.33 = (s32[]{:T(128)}, f32[16,16384]{1,0:T(8,128)S(1)}, s32[4]{0:T(128)S(1)}, s32[128]{0:T(128)}, bf16[128,128,128]{2,1,0:T(8,128)(2,1)}, /*index=5*/s32[1...) while((s32[]{:T(128)}, f32[16,16384]{1,0:T(8,128)S(1)}, ...), condition=%wide.region_3.4_spmd.clone, body=%wide.region_2.3_spmd.clone.sunk | while | flops 235931328 | bytes 10490993 | solution.py:34
  131.9 6.4 copy.22
  139.6 3.7 multiply_reduce_fusion
  143.4 16.6 %all-reduce = f32[2048]{0:T(1024)S(1)} all-reduce(f32[2048]{0:T(1024)S(1)} %convolution_bitcast_fusion.1), channel_id=2, replica_groups=mesh['row'=32,'col'=8] {'col'}, use_global_device_ids=true, to_apply=%region_1.2.clone | all-reduce | flops 2048 | bytes 16384
  160.3 4.7 reduce-scatter.4.cloned.1.call-done
  167.1 81.7 %all-gather.6.cloned.1.call-done = bf16[8192,256]{1,0:T(8,128)(2,1)} async-done(((bf16[256,256]{1,0:T(8,128)(2,1)}), bf16[8192,256]{1,0:T(8,128)(2,1)}) %all-gather.6.cloned.1.call-update) | async-done | bytes 4194320 | tf_op jit(solution)/shard_map/all_gather | solution.py:81
  248.8 56.9 %while.34 = (s32[]{:T(128)}, f32[16,32768]{1,0:T(8,128)}, s32[4]{0:T(128)S(1)}, s32[128]{0:T(128)S(1)}, bf16[128,128,128]{2,1,0:T(8,128)(2,1)}, /*index=5*/s32[1...) while((s32[]{:T(128)}, f32[16,32768]{1,0:T(8,128)}, ...), condition=%wide.region_6.7_spmd.clone, body=%wide.region_5.6_spmd.clone.sunk | while | flops 471860928 | bytes 45094056 | solution.py:34
  251.5 2.9 gather_fusion.1
  258.8 2.8 convolution_add_fusion.10
  265.7 2.9 gather_fusion.1
  273.0 2.8 convolution_add_fusion.10
  279.9 2.9 gather_fusion.1
  287.3 2.8 convolution_add_fusion.10
  294.2 2.9 gather_fusion.1
  301.5 2.8 convolution_add_fusion.10
  305.7 2.7 reshape.84
  309.6 32.5 %reduce-scatter.6.cloned.1.call-done = f32[256,256]{1,0:T(8,128)} async-done(((f32[2048,256]{1,0:T(8,128)}), f32[256,256]{1,0:T(8,128)}) %reduce-scatter.6.cloned.1.call-update) | async-done | bytes 262160 | tf_op jit(solution)/shard_map/reduce_scatter | solution.py:83
  344.8 27.6 %all-gather.8.cloned.1.call-done = bf16[2048,256]{1,0:T(8,128)(2,1)} async-done(((bf16[256,256]{1,0:T(8,128)(2,1)}), bf16[2048,256]{1,0:T(8,128)(2,1)}) %all-gather.8.cloned.1.call-update) | async-done | bytes 1048592 | tf_op jit(solution)/shard_map/all_gather | solution.py:100
  372.3 75.5 %while.35 = (s32[]{:T(128)}, f32[64,32768]{1,0:T(8,128)}, s32[4]{0:T(128)S(1)}, s32[128]{0:T(128)S(1)}, bf16[128,128,128]{1,2,0:T(8,128)(2,1)}, /*index=5*/s32[1...) while((s32[]{:T(128)}, f32[64,32768]{1,0:T(8,128)}, ...), condition=%wide.region_11.12_spmd.clone, body=%wide.region_10.11_spmd.clone.sunk | while | flops 1078988032 | bytes 99620024 | solution.py:34
  381.6 6.4 convolution_add_fusion.11
  388.0 3.2 copy-done.2
  400.5 6.4 convolution_add_fusion.11
  406.9 3.2 copy-done.2
  419.3 6.4 convolution_add_fusion.11
  425.7 3.2 copy-done.2
  438.2 6.4 convolution_add_fusion.11
  444.6 3.2 copy-done.2
  447.8 9.3 reshape.86
  459.0 223.2 %reduce-scatter.8.cloned.1.call-done = f32[256,256]{1,0:T(8,128)} async-done(((f32[8192,256]{1,0:T(8,128)}), f32[256,256]{1,0:T(8,128)}) %reduce-scatter.8.cloned.1.call-update) | async-done | bytes 262160 | tf_op jit(solution)/shard_map/reduce_scatter | solution.py:102
  685.3 78.5 %all-reduce.1 = (f32[256]{0:T(256)}, f32[172]{0:T(256)}) all-reduce(f32[256]{0:T(256)S(1)} %get-tuple-element.313, f32[172]{0:T(256)S(1)} %get-tuple-element.307), channel_id=1, replica_groups=mesh['row'=32,'col'=8] {'row','col'}, use_global_device_ids=true, to_apply=%region_16.17 | all-reduce | flops 428 | bytes 3424 | tf_op jit(solution)/shard_map/psum | solution.py:120
  763.8 180.5 %all-reduce.5.cloned.1.call-done = (f32[128,256]{0,1:T(8,128)}, f32[128,256]{1,0:T(8,128)}, f32[256,172]{0,1:T(8,128)}, f32[256,172]{0,1:T(8,128)}) async-done(((f32[128,256]{0,1:T(8,128)}, f32[128,256]{1,0:T(8,128)}, f32[256,172]{0,1:T(8,128)}, f32[256,172]{0,1:T(8,128)}), (f32[128,256]{0,1:T(8,128)}, f32[128,256]{1,0:T(8,128)}, f32[256,172]{0,1:T(8,128)}, ...) | async-done | bytes 614416 | tf_op jit(solution)/shard_map/psum | solution.py:120
  (191 shorter events, 109.7 us)
Async XLA Ops:
  7.2 334.9 %copy-start = (bf16[256,172]{0,1:T(8,128)(2,1)S(1)}, bf16[256,172]{0,1:T(8,128)(2,1)}, u32[]{:S(2)}) copy-start(bf16[256,172]{0,1:T(8,128)(2,1)} %param.28) | copy-start | bytes 264196
  7.2 81.3 %all-gather.4.cloned.1.call-start = ((), (), s32[]{:S(2)}) async-start(), calls=%async_computation.3 | async-start | bytes 2162688 | tf_op jit(solution)/shard_map/all_gather | solution.py:62
  7.9 157.1 %reduce-scatter.4.cloned.1.call-start = ((), (), s32[]{:S(2)}) async-start(), calls=%async_computation.4 | async-start | bytes 1179648 | tf_op jit(solution)/shard_map/reduce_scatter | solution.py:70
  131.8 116.9 %all-gather.6.cloned.1.call-start = ((), (), s32[]{:S(2)}) async-start(), calls=%async_computation.5 | async-start | bytes 4325376 | tf_op jit(solution)/shard_map/all_gather | solution.py:81
  131.9 6.4 copy-start.18
  139.5 3.8 copy-start.13
  139.5 20.6 %copy-start.7 = (bf16[256,128]{1,0:T(8,128)(2,1)S(1)}, bf16[256,128]{1,0:T(8,128)(2,1)}, u32[]{:S(2)}) copy-start(bf16[256,128]{1,0:T(8,128)(2,1)} %param.18) | copy-start | bytes 196612
  139.5 20.6 %copy-start.10 = (bf16[128,256]{1,0:T(8,128)(2,1)S(1)}, bf16[128,256]{1,0:T(8,128)(2,1)}, u32[]{:S(2)}) copy-start(bf16[128,256]{1,0:T(8,128)(2,1)} %param.24) | copy-start | bytes 196612
  139.6 25.5 %copy-start.11 = (bf16[128,256]{1,0:T(8,128)(2,1)S(1)}, bf16[128,256]{1,0:T(8,128)(2,1)}, u32[]{:S(2)}) copy-start(bf16[128,256]{1,0:T(8,128)(2,1)} %param.25) | copy-start | bytes 196612
  139.6 25.5 %copy-start.14 = (f32[256]{0:T(256)S(1)}, f32[256]{0:T(256)}, u32[]{:S(2)}) copy-start(f32[256]{0:T(256)} %param.26) | copy-start | bytes 3076
  139.6 109.2 %copy-start.12 = (s32[128]{0:T(128)S(1)}, s32[128]{0:T(128)}, u32[]{:S(2)}) copy-start(s32[128]{0:T(128)} %get-tuple-element.595) | copy-start | bytes 1540
  166.9 175.2 %reduce-scatter.6.cloned.1.call-start = ((), (), s32[]{:S(2)}) async-start(), calls=%async_computation.6 | async-start | bytes 2359296 | tf_op jit(solution)/shard_map/reduce_scatter | solution.py:83
  270.6 2.4 copy-start.3
  308.4 33.7 %copy-start.15 = (f32[172]{0:T(256)S(1)}, f32[172]{0:T(256)}, u32[]{:S(2)}) copy-start(f32[172]{0:T(256)} %param.29) | copy-start | bytes 2068
  308.4 35.0 %copy-start.16 = (s32[256]{0:T(256)S(1)}, s32[256]{0:T(256)}, u32[]{:S(2)}) copy-start(s32[256]{0:T(256)} %param.22) | copy-start | bytes 3076
  308.5 63.9 %all-gather.8.cloned.1.call-start = ((), (), s32[]{:S(2)}) async-start(), calls=%async_computation.7 | async-start | bytes 1179648 | tf_op jit(solution)/shard_map/all_gather | solution.py:100
  344.5 337.8 %reduce-scatter.8.cloned.1.call-start = ((), (), s32[]{:S(2)}) async-start(), calls=%async_computation.8 | async-start | bytes 8650752 | tf_op jit(solution)/shard_map/reduce_scatter | solution.py:102
  376.9 4.6 slice-start
  379.1 2.5 slice-start.1
  388.0 3.2 copy-start.2
  395.8 4.6 slice-start
  398.0 2.5 slice-start.1
  406.9 3.2 copy-start.2
  414.7 4.6 slice-start
  416.9 2.5 slice-start.1
  425.7 3.2 copy-start.2
  433.6 4.6 slice-start
  435.7 2.5 slice-start.1
  444.6 3.2 copy-start.2
  457.2 227.2 %copy-start.8 = (f32[256,128]{1,0:T(8,128)S(1)}, f32[256,128]{1,0:T(8,128)}, u32[]{:S(2)}) copy-start(f32[256,128]{1,0:T(8,128)} %reduce-scatter.4.cloned.1.call-done) | copy-start | bytes 393220
  457.2 493.6 %copy-start.1 = (bf16[256,172]{0,1:T(8,128)(2,1)S(1)}, bf16[256,172]{0,1:T(8,128)(2,1)}, u32[]{:S(2)}) copy-start(bf16[256,172]{0,1:T(8,128)(2,1)} %param.28) | copy-start | bytes 264196
  457.2 487.1 %all-reduce.5.cloned.1.call-start = ((), (), s32[]{:S(2)}) async-start(), calls=%async_computation.9 | async-start | bytes 1245184 | tf_op jit(solution)/shard_map/psum | solution.py:120
  (11 other events, 16.4 us)
Sparse Core Ops, SparseCore 0:
  10.6 77.8 all-gather.3
  132.0 33.0 reduce-scatter.3
  168.2 80.5 all-gather.5
  308.6 33.4 reduce-scatter.5
  344.6 27.6 all-gather.7
  457.3 224.9 reduce-scatter.7
  689.9 254.3 all-reduce.4
where the time goes:
time: 960 us; the launch traced here: 958 us
  waiting for transfers between devices  631 us (66%)
  local copies, waits for them, and re-layouts  104 us (11%)
  blocking collectives  95.2 us (10%)
  matrix products  79.2 us (8%)
  loops' own time  24 us (2%)
  between operations  15 us (2%)
    reduce_scatter x1, waiting for transfers between devices, on_device(): lax.psum_scatter(backflow_part, 'row', scatter_dimension=0, tiled=True)  223 us
    psum x1, waiting for transfers between devices, on_device(): lax.psum((local_grads[0], local_grads[1], local_grads[2], local_grads[3],...  180 us
    all_gather x1, waiting for transfers between devices, on_device(): hidden_rows = lax.all_gather(hidden, 'row', axis=0, tiled=True)  81.7 us
    all_gather x1, waiting for transfers between devices, on_device(): gathered = lax.all_gather(features, 'row', axis=0, tiled=True)  80.5 us
    psum x1, blocking collectives, on_device(): lax.psum((local_grads[0], local_grads[1], local_grads[2], local_grads[3],...  78.5 us
    dot_general x12, matrix products, add_group(): jnp.dot(selector, product.reshape(group_size, tile_edge * columns), preci...  46.4 us
    while x48, local copies, waits for them, and re-layouts  37.9 us
    reduce_scatter x1, waiting for transfers between devices, on_device(): lax.psum_scatter(second_part, 'col', scatter_dimension=0, tiled=True)  32.5 us
  transfers between devices with their start and end apart: 7, of which 7 were waited for; matrix products, arithmetic and copies ran while one was open for 1% of the time, Pallas kernels for 0%

commit v1 on v0

v1 whole, which is shorter than its diff:
```python
import functools
import math

import jax
import jax.numpy as jnp
from jax import lax
from jax.experimental import pallas as pl
from jax.experimental.pallas import tpu as pltpu
from jax.sharding import PartitionSpec as P

EDGE = 128
PAD = 176
NY, NZ = 4, 8
F32, BF16 = jnp.float32, jnp.bfloat16
VMEM = pl.BlockSpec(memory_space=pltpu.VMEM)
SMEM = pl.BlockSpec(memory_space=pltpu.SMEM)
ANY = pl.BlockSpec(memory_space=pl.ANY)
NT = (((1,), (1,)), ((), ()))


def dot(a, b):
    return jnp.dot(a, b, preferred_element_type=F32)


def dot_nt(a, b):
    return lax.dot_general(a, b, NT, preferred_element_type=F32)


def call(body, out, n_smem, n_in, scratch=(), any_from=None, flops=0, bytes_accessed=0):
    specs = [SMEM] * n_smem + [VMEM] * (n_in - n_smem)
    if any_from is not None:
        specs[any_from:] = [ANY] * (n_in - any_from)
    return pl.pallas_call(
        body,
        out_shape=out,
        in_specs=specs,
        out_specs=jax.tree.map(lambda _: VMEM, out),
        scratch_shapes=list(scratch),
        compiler_params=pltpu.CompilerParams(vmem_limit_bytes=48 * 1024 * 1024),
        cost_estimate=pl.CostEstimate(
            flops=flops, bytes_accessed=bytes_accessed, transcendentals=0
        ),
    )


def step(x, groups, shift):
    pairs = [(g[i], g[(i + shift) % len(g)]) for g in groups for i in range(len(g))]
    return lax.ppermute(x, "row", pairs)


def gather_rows(x):
    along_z = [[NZ * y + z for z in range(NZ)] for y in range(NY)]
    along_y = [[NZ * y + z for y in range(NY)] for z in range(NZ)]
    x = jnp.concatenate(
        [x, step(x, along_y, 1), step(x, along_y, -1), step(x, along_y, 2)], axis=0
    )
    up = down = x
    parts = [x]
    for _ in range(NZ // 2 - 1):
        up, down = step(up, along_z, 1), step(down, along_z, -1)
        parts += [up, down]
    half = x.shape[0] // 2
    parts += [step(up[:half], along_z, 1), step(down[half:], along_z, -1)]
    return parts


def place_of(block, row):
    owner = block // 2
    dz = (owner % NZ - row % NZ) % NZ
    dy = (owner // NZ - row // NZ) % NY
    z_place = jnp.where(dz <= 3, 2 * dz, jnp.where(dz == 4, 7, 15 - 2 * dz))
    y_place = jnp.where(dy == 0, 0, jnp.where(dy == 3, 1, dy + 1))
    return (z_place * NY + y_place) * 2 + block % 2


def block_at(place, row):
    z_place, y_place = place // (2 * NY), place // 2 % NY
    dz = jnp.where(z_place == 7, 4, jnp.where(z_place % 2 == 0, z_place // 2, 8 - (z_place + 1) // 2))
    dy = jnp.where(y_place == 0, 0, jnp.where(y_place == 1, 3, y_place - 1))
    z = (row % NZ + dz) % NZ
    y = (row // NZ + dy) % NY
    return (y * NZ + z) * 2 + place % 2


def start_parts(parts, held, sem):
    copies, at = [], 0
    for p in parts:
        n = p.shape[0]
        copies.append(pltpu.make_async_copy(p, held.at[pl.ds(at, n)], sem.at[len(copies)]))
        copies[-1].start()
        at += n
    return copies


def degree_kernel(rows, tiles, out):
    out[...] = jnp.zeros_like(out)
    ones = jnp.ones((8, EDGE), BF16)

    def body(t, carry):
        x = tiles[t].astype(F32)
        x = x * x
        hi = x.astype(BF16)
        lo = (x - hi.astype(F32)).astype(BF16)
        out[rows[t]] += dot_nt(ones, hi) + dot_nt(ones, lo)
        return carry

    lax.fori_loop(0, tiles.shape[0], body, 0, unroll=4)


def first_kernel(n_parts, offs, cols, tiles, deg, *refs):
    parts, out, held, sem = refs[:n_parts], refs[n_parts], refs[n_parts + 1], refs[n_parts + 2]
    copies = start_parts(parts, held, sem)
    out[...] = jnp.zeros_like(out)
    for g in range(8):
        for b in range(2):
            out[pl.ds(g * 264 + 256 + b, 1), :] = deg[2 * g + b][:1]
    for c in copies:
        c.wait()
    unroll = 4

    def body(i, carry):
        got = [dot(tiles[i * unroll + u], held[cols[i * unroll + u]]) for u in range(unroll)]
        for u in range(unroll):
            at = pl.ds(pl.multiple_of(offs[i * unroll + u], 8), EDGE)
            out[at, :] += got[u]
        return carry

    lax.fori_loop(0, tiles.shape[0] // unroll, body, 0)


def hidden_kernel(sums, features, self_first, neigh_first, bias, agg, hid, inv):
    total = sums[0]
    for g in range(1, 8):
        total = total + sums[g]
    for b in range(2):
        x = 1.0 + total[256 + b : 257 + b]
        r = lax.rsqrt(x)
        r = r * (1.5 - 0.5 * x * r * r)
        inv[pl.ds(b, 1), :] = r
        column = jnp.broadcast_to(r, (EDGE, EDGE)).T
        agg[b] = (column * total[b * EDGE : (b + 1) * EDGE]).astype(BF16)
        pre = (
            dot_nt(self_first[...], features[b])
            + dot_nt(neigh_first[...], agg[b])
            + bias[...]
        )
        hid[b] = jnp.maximum(pre, 0.0).astype(BF16)


def second_kernel(n_parts, rows, cols, tiles, neigh, *refs):
    parts, agg, logit, held, acc, sem = refs[:n_parts], *refs[n_parts:]
    copies = start_parts(parts, held, sem)
    acc[...] = jnp.zeros_like(acc)
    for c in copies:
        c.wait()
    unroll = 2

    def body(i, carry):
        got = [dot_nt(held[cols[i * unroll + u]], tiles[i * unroll + u]) for u in range(unroll)]
        for u in range(unroll):
            acc[rows[i * unroll + u]] += got[u]
        return carry

    lax.fori_loop(0, tiles.shape[0] // unroll, body, 0)

    def finish(d, carry):
        agg[d] = acc[d].astype(BF16)
        logit[d] = dot(neigh[...], agg[d]).astype(BF16)
        return carry

    lax.fori_loop(0, 16, finish, 0, unroll=2)


def loss_kernel(classes, scale, parts, hid, self_t, bias, labels, mask, inv, lg, w, grad, grad_bias):
    rows = lax.broadcasted_iota(jnp.int32, (PAD, EDGE), 0)
    ones = jnp.ones((8, EDGE), BF16)
    for b in range(2):
        total = parts[0, b].astype(F32)
        for g in range(1, 8):
            total = total + parts[g, b].astype(F32)
        factor = inv[b : b + 1]
        logits = dot(self_t[...], hid[b]) + factor * total + bias[...]
        logits = jnp.where(rows < classes, logits, -1e30)
        e = jnp.exp(logits - jnp.max(logits, axis=0, keepdims=True))
        p = e / jnp.sum(e, axis=0, keepdims=True)
        p = p - jnp.where(rows == labels[b : b + 1], 1.0, 0.0)
        got = (p * (mask[b : b + 1].astype(F32) * scale)).astype(BF16)
        lg[b] = got
        w[b] = (got.astype(F32) * factor).astype(BF16)
        if b == 0:
            grad[...] = dot_nt(got, hid[b])
            grad_bias[...] = dot_nt(ones, got)
        else:
            grad[...] += dot_nt(got, hid[b])
            grad_bias[...] += dot_nt(ones, got)


def last_kernel(
    n_parts, rows, cols, order, tiles, w, agg_second, lg, self_second, neigh_second,
    grad_self, grad_bias, feat, agg_first, *refs
):
    parts, out, held, acc, proj, g_neigh, g_first, g_bias, sem = refs[:n_parts], *refs[n_parts:]
    copies = start_parts(parts, held, sem)

    def project(d, carry):
        proj[d] = dot(neigh_second[...], w[d]).astype(BF16)
        got = dot_nt(w[d], agg_second[d])
        g_neigh[...] = jnp.where(d == 0, 0.0, g_neigh[...]) + got
        return carry

    g_neigh[...] = jnp.zeros_like(g_neigh)
    lax.fori_loop(0, 16, project, 0)
    acc[...] = jnp.zeros_like(acc)
    for b in range(2):
        acc[b] = dot(self_second[...], lg[b])
    unroll = 2

    def body(i, carry):
        got = [dot(proj[rows[i * unroll + u]], tiles[i * unroll + u]) for u in range(unroll)]
        for u in range(unroll):
            acc[cols[i * unroll + u]] += got[u]
        return carry

    lax.fori_loop(0, tiles.shape[0] // unroll, body, 0)
    for c in copies:
        c.wait()
    ones = jnp.ones((8, EDGE), BF16)
    g_first[...] = jnp.zeros_like(g_first)
    g_bias[...] = jnp.zeros_like(g_bias)

    def contract(s, carry):
        p = jnp.where(held[s].astype(F32) > 0.0, acc[s], 0.0).astype(BF16)
        g_first[0] += dot(p, feat[s])
        g_first[1] += dot(p, agg_first[order[s]])
        g_bias[...] += dot_nt(ones, p)
        return carry

    lax.fori_loop(0, 64, contract, 0)
    out[pl.ds(0, 256), :] = g_first[0].astype(BF16)
    out[pl.ds(256, 256), :] = g_first[1].astype(BF16)
    for i in range(2):
        lanes = slice(i * EDGE, (i + 1) * EDGE)
        out[pl.ds(512 + i * PAD, PAD), :] = grad_self[:, lanes].astype(BF16)
        out[pl.ds(512 + (2 + i) * PAD, PAD), :] = g_neigh[:, lanes].astype(BF16)
    pick = lax.broadcasted_iota(jnp.int32, (16, EDGE), 0)
    zeros = jnp.zeros((1, 256 - PAD), F32)
    second = jnp.concatenate([grad_bias[:1], zeros], axis=1)
    last = jnp.where(
        pick == 0,
        g_bias[:1, :EDGE],
        jnp.where(
            pick == 1,
            g_bias[:1, EDGE:],
            jnp.where(pick == 2, second[:, :EDGE], jnp.where(pick == 3, second[:, EDGE:], 0.0)),
        ),
    )
    out[pl.ds(512 + 4 * PAD, 16), :] = last.astype(BF16)
    out[pl.ds(512 + 4 * PAD + 16, 1280 - 528 - 4 * PAD), :] = jnp.zeros(
        (1280 - 528 - 4 * PAD, EDGE), BF16
    )


def on_device(
    features,
    tiles,
    block_rows,
    block_cols,
    labels,
    train_mask,
    self_first,
    neigh_first,
    bias_first,
    self_second,
    neigh_second,
    bias_second,
):
    classes = self_second.shape[1]
    hid_size = self_first.shape[1]
    scale = 1.0 / math.sqrt(65536)
    row = lax.axis_index("row")
    tiles = tiles.reshape(-1, EDGE, EDGE)
    rows = block_rows.reshape(-1)
    cols = place_of(block_cols.reshape(-1), row)
    offs = rows // 2 * 264 + rows % 2 * EDGE
    order = block_at(jnp.arange(64, dtype=jnp.int32), row)
    shape = jax.ShapeDtypeStruct
    feat = features.reshape(2, EDGE, EDGE)

    feat_parts = gather_rows(feat)
    n_parts = len(feat_parts)
    sems = pltpu.SemaphoreType.DMA((n_parts,))
    deg = call(degree_kernel, shape((16, 8, EDGE), F32), 1, 2, flops=2**28, bytes_accessed=2**22)(
        rows, tiles
    )
    first = call(
        functools.partial(first_kernel, n_parts),
        shape((8 * 264, EDGE), F32),
        2,
        4 + n_parts,
        [pltpu.VMEM((64, EDGE, EDGE), BF16), sems],
        any_from=4,
        flops=2**29,
        bytes_accessed=2**23,
    )(offs, cols, tiles, deg, *feat_parts)
    sums = lax.all_to_all(first.reshape(8, 264, EDGE), "col", 0, 0, tiled=True)
    agg, hid, inv = call(
        hidden_kernel,
        (
            shape((2, EDGE, EDGE), BF16),
            shape((2, hid_size, EDGE), BF16),
            shape((2, EDGE), F32),
        ),
        0,
        5,
    )(
        sums,
        feat,
        self_first.T,
        neigh_first.T,
        jnp.broadcast_to(bias_first[:, None], (hid_size, EDGE)),
    )
    hid_parts = gather_rows(hid)
    agg_first = lax.all_gather(agg, "row", axis=0, tiled=True)

    wide = ((0, 0), (0, PAD - classes))
    self_wide = jnp.pad(self_second, wide)
    neigh_wide = jnp.pad(neigh_second, wide)
    bias_wide = jnp.broadcast_to(jnp.pad(bias_second, (0, PAD - classes))[:, None], (PAD, EDGE))
    agg_second, partial = call(
        functools.partial(second_kernel, n_parts),
        (shape((16, hid_size, EDGE), BF16), shape((16, PAD, EDGE), BF16)),
        2,
        4 + n_parts,
        [pltpu.VMEM((64, hid_size, EDGE), BF16), pltpu.VMEM((16, hid_size, EDGE), F32), sems],
        any_from=4,
        flops=2**30,
        bytes_accessed=2**23,
    )(rows, cols, tiles, neigh_wide.T, *hid_parts)
    partial = lax.all_to_all(partial.reshape(8, 2, PAD, EDGE), "col", 0, 0, tiled=True)
    lg, w, grad_self, grad_bias = call(
        functools.partial(loss_kernel, classes, scale),
        (
            shape((2, PAD, EDGE), BF16),
            shape((2, PAD, EDGE), BF16),
            shape((PAD, hid_size), F32),
            shape((8, PAD), F32),
        ),
        0,
        7,
    )(
        partial,
        hid,
        self_wide.T,
        bias_wide,
        labels.reshape(2, EDGE),
        train_mask.reshape(2, EDGE),
        inv,
    )
    w_all = lax.all_gather(w, "col", axis=0, tiled=True)
    grads = call(
        functools.partial(last_kernel, n_parts),
        shape((1280, EDGE), BF16),
        3,
        13 + n_parts,
        [
            pltpu.VMEM((64, hid_size, EDGE), BF16),
            pltpu.VMEM((64, hid_size, EDGE), F32),
            pltpu.VMEM((16, hid_size, EDGE), BF16),
            pltpu.VMEM((PAD, hid_size), F32),
            pltpu.VMEM((2, hid_size, EDGE), F32),
            pltpu.VMEM((8, hid_size), F32),
            sems,
        ],
        any_from=13,
        flops=2**31,
        bytes_accessed=2**24,
    )(
        rows, cols, order, tiles, w_all, agg_second, lg, self_wide, neigh_wide,
        grad_self, grad_bias, jnp.concatenate(feat_parts, axis=0), agg_first, *hid_parts
    )
    every = ("row", "col")
    mine = lax.all_to_all(grads.reshape(256, 5, EDGE), every, 0, 0, tiled=True)
    mine = jnp.sum(mine.astype(F32), axis=0).astype(BF16)
    full = lax.all_to_all(jnp.broadcast_to(mine[None], (256, 5, EDGE)), every, 0, 0, tiled=True)
    full = full.reshape(1280, EDGE).astype(F32)
    half = lambda at, n: jnp.concatenate([full[at : at + n], full[at + PAD : at + PAD + n]], axis=1)
    end = 512 + 4 * PAD
    return (
        full[:256].T,
        full[256:512].T,
        full[end : end + 2].reshape(hid_size),
        half(512, classes).T,
        half(512 + 2 * PAD, classes).T,
        full[end + 2 : end + 4].reshape(256)[:classes],
    )


def solution(mesh):
    in_specs = (
        P(("row", "col"), None),
        P("row", "col", None, None, None),
        P("row", "col", None),
        P("row", "col", None),
        P(("row", "col")),
        P(("row", "col")),
        P(),
        P(),
        P(),
        P(),
        P(),
        P(),
    )
    out_specs = (P(), P(), P(), P(), P(), P())
    return jax.shard_map(
        on_device, mesh=mesh, in_specs=in_specs, out_specs=out_specs, check_vma=False
    )
```

time: 960 us -> 312 us (0.33)
  waiting for transfers between devices: 631 us -> 62.6 us
  matrix products: 79.2 us -> 0 us
  Pallas kernels: 0 us -> 69.9 us
  local copies, waits for them, and re-layouts: 104 us -> 36.3 us
  starting transfers between devices: 0.69 us -> 52.7 us
  loops' own time: 24 us -> 0 us
  blocking collectives: 95.2 us -> 72.1 us
    reduce_scatter x3 -> x0, waiting for transfers between devices: 260 us -> none  [the longest x1 223 us: on_device(): lax.psum_scatter(backflow_part, 'row', scatter_dimension=0, tiled=True)]
    all_gather x3 -> x1, waiting for transfers between devices: 190 us -> 0.01 us  [on_device(): agg_first = lax.all_gather(agg, 'row', axis=0, tiled=True)]
    psum x1 -> x0, waiting for transfers between devices: 180 us -> none  [on_device(): lax.psum((local_grads[0], local_grads[1], local_grads[2], local_grads[3],...]
    dot_general x35 -> x0, matrix products: 79.2 us -> none  [the longest x12 46.4 us: add_group(): jnp.dot(selector, product.reshape(group_size, tile_edge * columns), preci...]
    psum x1 -> x0, blocking collectives: 78.5 us -> none  [on_device(): lax.psum((local_grads[0], local_grads[1], local_grads[2], local_grads[3],...]
    pallas_call x0 -> x6, Pallas kernels: none -> 69.9 us  [the longest x1 31.6 us: on_device(): call(functools.partial(last_kernel, n_parts), shape((1280, EDGE), BF16),...]
    all_to_all x0 -> x2, blocking collectives: none -> 58.1 us  [the longest x1 32.1 us: on_device(): mine = lax.all_to_all(grads.reshape(256, 5, EDGE), every, 0, 0, tiled=True)]
    ppermute x0 -> x22, waiting for transfers between devices: none -> 45.6 us  [step(): return lax.ppermute(x, 'row', pairs)]
  transfers between devices with their start and end apart: 7 -> 25, of which waited for: 7 -> 16; matrix products, arithmetic and copies ran while one was open for 1% -> 6% of each run, Pallas kernels for 0% -> 9%
where the time goes in v1:
time: 312 us; the launch traced here: 311 us
  blocking collectives  72.1 us (23%)
  Pallas kernels  69.9 us (22%)
  waiting for transfers between devices  62.6 us (20%)
  starting transfers between devices  52.7 us (17%)
  local copies, waits for them, and re-layouts  36.3 us (12%)
  between operations  14.6 us (5%)
    ppermute x22, waiting for transfers between devices, step(): return lax.ppermute(x, 'row', pairs)  45.6 us
    ppermute x22, starting transfers between devices, step(): return lax.ppermute(x, 'row', pairs)  32.6 us
    all_to_all x1, blocking collectives, on_device(): mine = lax.all_to_all(grads.reshape(256, 5, EDGE), every, 0, 0, tiled=True)  32.1 us
    pallas_call x1, Pallas kernels, on_device(): call(functools.partial(last_kernel, n_parts), shape((1280, EDGE), BF16),...  31.6 us
    unnamed x108, local copies, waits for them, and re-layouts  27.9 us
    all_to_all x1, blocking collectives, on_device(): lax.all_to_all(jnp.broadcast_to(mine[None], (256, 5, EDGE)), every, 0, 0,...  26 us
    pallas_call x1, Pallas kernels, on_device(): call(functools.partial(second_kernel, n_parts), (shape((16, hid_size, EDG...  18.2 us
    all_to_all x1, waiting for transfers between devices, on_device(): sums = lax.all_to_all(first.reshape(8, 264, EDGE), 'col', 0, 0, tiled=True)  15.2 us
  transfers between devices with their start and end apart: 25, of which 16 were waited for; matrix products, arithmetic and copies ran while one was open for 6% of the time, Pallas kernels for 9%

profile of v1, /device:TPU:1, one launch (start us, length us, event | category | flops | bytes accessed | tf_op | source)
XLA Modules:
  0.0 310.7 jit_solution(8274526464730357430)
XLA Ops:
  7.2 2.2 collective-permute-start
  12.7 3.1 %collective-permute-done.2 = bf16[2,128,128]{2,1,0:T(8,128)(2,1)S(1)} collective-permute-done((bf16[2,128,128]{2,1,0:T(8,128)(2,1)}, bf16[2,128,128]{2,1,0:T(8,128)(2,1)S(1)}, u32[]{:S(2)}, u32[]{:S(2)}) %collective-permute-start.2) | collective-permute-done | bytes 65568 | tf_op jit(solution)/shard_map/ppermute | solution.py:48
  18.3 4.0 %collective-permute-start.4 = (bf16[8,128,128]{2,1,0:T(8,128)(2,1)S(1)}, bf16[8,128,128]{2,1,0:T(8,128)(2,1)S(1)}, u32[]{:S(2)}, u32[]{:S(2)}) collective-permute-start(bf16[8,128,128]{2,1,0:T(8,128)(2,1)S(1)} %pad_maximum_fusion.refs_0_), channel_id=1, source_target_pairs={{0,56},{8,0},{16,8},{24,16},{32,24},{40,32},{48,40},{56,48},{64,12... | collective-permute-start | bytes 786440 | tf_op jit(solution)/shard_map/ppermute | solution.py:48
  22.4 4.3 %collective-permute-done.3.refs_1_ = bf16[8,128,128]{2,1,0:T(8,128)(2,1)S(1)} collective-permute-done((bf16[8,128,128]{2,1,0:T(8,128)(2,1)S(1)}, bf16[8,128,128]{2,1,0:T(8,128)(2,1)S(1)}, u32[]{:S(2)}, u32[]{:S(2)}) %collective-permute-start.3) | collective-permute-done | bytes 262176 | tf_op jit(solution)/shard_map/ppermute | solution.py:48
  26.7 2.7 collective-permute-start.6
  29.3 3.8 %collective-permute-done.5.refs_3_ = bf16[8,128,128]{2,1,0:T(8,128)(2,1)S(1)} collective-permute-done((bf16[8,128,128]{2,1,0:T(8,128)(2,1)S(1)}, bf16[8,128,128]{2,1,0:T(8,128)(2,1)S(1)}, u32[]{:S(2)}, u32[]{:S(2)}) %collective-permute-start.5) | collective-permute-done | bytes 262176 | tf_op jit(solution)/shard_map/ppermute | solution.py:48
  33.1 2.7 collective-permute-start.8
  35.9 2.2 copy-done
  38.7 8.8 %shard_map.163.deg = f32[16,8,128]{2,1,0:T(8,128)S(1)} custom-call(s32[128]{0:T(128)S(1)} %bitcast.53, bf16[128,128,128]{2,1,0:T(8,128)(2,1)S(1)} %bitcast.43), custom_call_target="tpu_custom_call" | custom-call | flops 268435456 | bytes 4194304 | tf_op jit(solution)/shard_map/pallas_call | solution.py:292
  47.7 2.7 collective-permute-start.10
  50.4 2.2 collective-permute-done.9.refs_7_
  52.7 9.9 %shard_map.164 = f32[2112,128]{1,0:T(8,128)} custom-call(s32[128]{0:T(128)S(1)} %get-tuple-element.55.offs, s32[128]{0:T(128)S(1)} %get-tuple-element.54.cols, bf16[128,128,128]{2,1,0:T(8,128)(2,1)} %bitcast.40, f32[16,8,128]{2,1,0:T(8,128)S(1)} %shard_map.163.deg, bf16[8,128,128]{2,1,0:T(8,128)(2,1)S(1)} %pad_maximum_fusion.refs_0_, ...), custom_call_target="tpu_custom_call" | custom-call | flops 536870912 | bytes 8388608 | tf_op jit(solution)/shard_map/pallas_call | solution.py:295
  62.6 10.2 %all-to-all-start = ((f32[8,264,128]{2,1,0:T(8,128)}), f32[8,264,128]{2,1,0:T(8,128)S(1)}, u32[]{:S(2)}, u32[]{:S(2)}) async-start(f32[8,264,128]{2,1,0:T(8,128)} %bitcast.5), calls=%async_computation | async-start | bytes 2162688 | tf_op jit(solution)/shard_map/all_to_all | solution.py:305
  73.1 15.2 %all-to-all-done.sums = f32[8,264,128]{2,1,0:T(8,128)S(1)} async-done(((f32[8,264,128]{2,1,0:T(8,128)}), f32[8,264,128]{2,1,0:T(8,128)S(1)}, u32[]{:S(2)}, u32[]{:S(2)}) %all-to-all-start) | async-done | bytes 1081376 | tf_op jit(solution)/shard_map/all_to_all | solution.py:305
  89.5 2.4 collective-permute-start.12
  92.4 2.2 collective-permute-done.11
  94.6 2.7 collective-permute-done.13
  97.7 3.1 collective-permute-start.15
  100.7 10.3 %collective-permute-done.14.refs_1_ = bf16[8,256,128]{2,1,0:T(8,128)(2,1)S(1)} collective-permute-done((bf16[8,256,128]{2,1,0:T(8,128)(2,1)S(1)}, bf16[8,256,128]{2,1,0:T(8,128)(2,1)S(1)}, u32[]{:S(2)}, u32[]{:S(2)}) %collective-permute-start.14) | collective-permute-done | bytes 524320 | tf_op jit(solution)/shard_map/ppermute | solution.py:48
  111.0 2.7 collective-permute-start.17
  116.0 7.3 %collective-permute-done.16.refs_3_ = bf16[8,256,128]{2,1,0:T(8,128)(2,1)S(1)} collective-permute-done((bf16[8,256,128]{2,1,0:T(8,128)(2,1)S(1)}, bf16[8,256,128]{2,1,0:T(8,128)(2,1)S(1)}, u32[]{:S(2)}, u32[]{:S(2)}) %collective-permute-start.16) | collective-permute-done | bytes 524320 | tf_op jit(solution)/shard_map/ppermute | solution.py:48
  124.2 2.0 collective-permute-start.19
  131.3 2.5 collective-permute-done.18.refs_5_
  134.5 2.2 collective-permute-start.21
  137.6 4.4 %collective-permute-done.20.refs_7_ = bf16[4,256,128]{2,1,0:T(8,128)(2,1)S(1)} collective-permute-done((bf16[4,256,128]{2,1,0:T(8,128)(2,1)S(1)}, bf16[4,256,128]{2,1,0:T(8,128)(2,1)S(1)}, u32[]{:S(2)}, u32[]{:S(2)}) %collective-permute-start.20) | collective-permute-done | bytes 262176 | tf_op jit(solution)/shard_map/ppermute | solution.py:48
  143.0 18.2 %shard_map.166 = (bf16[16,256,128]{2,1,0:T(8,128)(2,1)S(1)}, bf16[16,176,128]{2,1,0:T(8,128)(2,1)S(1)}) custom-call(s32[128]{0:T(128)S(1)} %bitcast.54, s32[128]{0:T(128)S(1)} %get-tuple-element.54.cols, bf16[128,128,128]{2,1,0:T(8,128)(2,1)} %bitcast.41, bf16[176,256]{1,0:T(8,128)(2,1)S(1)} %copy-done.23, ...), custom_call_target="tpu_custom_call" | custom-call | flops 1073741824 | bytes 8388608 | tf_op jit(solution)/shard_map/pallas_call | solution.py:329
  163.2 10.0 %all-to-all-start.1 = ((bf16[8,2,176,128]{3,2,1,0:T(8,128)(2,1)}), bf16[8,2,176,128]{3,2,1,0:T(8,128)(2,1)S(1)}, u32[]{:S(2)}, u32[]{:S(2)}) async-start(bf16[8,2,176,128]{3,2,1,0:T(8,128)(2,1)} %bitcast.44), calls=%async_computation.1 | async-start | bytes 1441792 | tf_op jit(solution)/shard_map/all_to_all | solution.py:339
  183.0 1.8 all-to-all-done.1.parts
  188.6 14.0 %all_gather.6.w = bf16[16,176,128]{2,1,0:T(8,128)(2,1)S(1)} all-gather(bf16[2,176,128]{2,1,0:T(8,128)(2,1)S(1)} %get-tuple-element.18), channel_id=1, replica_groups=mesh['row'=32,'col'=8] {'col'}, dimensions={0}, use_global_device_ids=true | all-gather | bytes 811008 | tf_op jit(solution)/shard_map/all_gather | solution.py:359
  208.3 31.6 %shard_map.168 = bf16[1280,128]{1,0:T(8,128)(2,1)S(1)} custom-call(s32[128]{0:T(128)S(1)} %bitcast.55, s32[128]{0:T(128)S(1)} %get-tuple-element.54.cols, s32[64]{0:T(128)S(1)} %fusion.order, bf16[128,128,128]{2,1,0:T(8,128)(2,1)} %bitcast.42, bf16[16,176,128]{2,1,0:T(8,128)(2,1)S(1)} %all_gather.6.w, bf16[16,256,128]{2,1,0:T(8,128)(2,1)} %copy-done.14, ...), custom_call_target="tpu_custom_call" | custom-call | flops 2147483648 | bytes 16777216 | tf_op jit(solution)/shard_map/pallas_call | solution.py:360
  241.8 32.1 %all_to_all.20 = bf16[256,5,128]{2,1,0:T(8,128)(2,1)S(1)} all-to-all(bf16[256,5,128]{2,1,0:T(8,128)(2,1)S(1)} %reshape.59), channel_id=1, replica_groups=mesh['row'=32,'col'=8] {'row','col'}, dimensions={0} | all-to-all | bytes 655360 | tf_op jit(solution)/shard_map/all_to_all | solution.py:382
  274.3 26.0 %all_to_all.21 = bf16[256,5,128]{2,1,0:T(8,128)(2,1)S(1)} all-to-all(bf16[256,5,128]{2,1,0:T(8,128)(2,1)S(1)} %broadcast_in_dim.28), channel_id=1, replica_groups=mesh['row'=32,'col'=8] {'row','col'}, dimensions={0} | all-to-all | bytes 655360 | tf_op jit(solution)/shard_map/all_to_all | solution.py:384
  (161 shorter events, 46.9 us)
Async XLA Ops:
  7.2 5.5 %collective-permute-start = (bf16[2,128,128]{2,1,0:T(8,128)(2,1)}, bf16[2,128,128]{2,1,0:T(8,128)(2,1)S(1)}, u32[]{:S(2)}, u32[]{:S(2)}) collective-permute-start(bf16[2,128,128]{2,1,0:T(8,128)(2,1)} %bitcast.45), channel_id=1, source_target_pairs={{0,64},{64,128},{128,192},{192,0},{8,72},{72,136},{136,200},{200,8... | collective-permute-start | bytes 196616 | tf_op jit(solution)/shard_map/ppermute | solution.py:48
  9.4 3.3 %collective-permute-start.1 = (bf16[2,128,128]{2,1,0:T(8,128)(2,1)}, bf16[2,128,128]{2,1,0:T(8,128)(2,1)S(1)}, u32[]{:S(2)}, u32[]{:S(2)}) collective-permute-start(bf16[2,128,128]{2,1,0:T(8,128)(2,1)} %bitcast.46), channel_id=1, source_target_pairs={{0,192},{64,0},{128,64},{192,128},{8,200},{72,8},{136,72},{200,136... | collective-permute-start | bytes 196616 | tf_op jit(solution)/shard_map/ppermute | solution.py:48
  10.9 4.9 %collective-permute-start.2 = (bf16[2,128,128]{2,1,0:T(8,128)(2,1)}, bf16[2,128,128]{2,1,0:T(8,128)(2,1)S(1)}, u32[]{:S(2)}, u32[]{:S(2)}) collective-permute-start(bf16[2,128,128]{2,1,0:T(8,128)(2,1)} %bitcast.47), channel_id=1, source_target_pairs={{0,128},{64,192},{128,0},{192,64},{8,136},{72,200},{136,8},{200,72... | collective-permute-start | bytes 196616 | tf_op jit(solution)/shard_map/ppermute | solution.py:48
  16.7 9.9 %collective-permute-start.3 = (bf16[8,128,128]{2,1,0:T(8,128)(2,1)S(1)}, bf16[8,128,128]{2,1,0:T(8,128)(2,1)S(1)}, u32[]{:S(2)}, u32[]{:S(2)}) collective-permute-start(bf16[8,128,128]{2,1,0:T(8,128)(2,1)S(1)} %pad_maximum_fusion.refs_0_), channel_id=1, source_target_pairs={{0,8},{8,16},{16,24},{24,32},{32,40},{40,48},{48,56},{56,0},{64,72... | collective-permute-start | bytes 786440 | tf_op jit(solution)/shard_map/ppermute | solution.py:48
  18.3 8.3 %collective-permute-start.4 = (bf16[8,128,128]{2,1,0:T(8,128)(2,1)S(1)}, bf16[8,128,128]{2,1,0:T(8,128)(2,1)S(1)}, u32[]{:S(2)}, u32[]{:S(2)}) collective-permute-start(bf16[8,128,128]{2,1,0:T(8,128)(2,1)S(1)} %pad_maximum_fusion.refs_0_), channel_id=1, source_target_pairs={{0,56},{8,0},{16,8},{24,16},{32,24},{40,32},{48,40},{56,48},{64,12... | collective-permute-start | bytes 786440 | tf_op jit(solution)/shard_map/ppermute | solution.py:48
  26.7 6.4 %collective-permute-start.5 = (bf16[8,128,128]{2,1,0:T(8,128)(2,1)S(1)}, bf16[8,128,128]{2,1,0:T(8,128)(2,1)S(1)}, u32[]{:S(2)}, u32[]{:S(2)}) collective-permute-start(bf16[8,128,128]{2,1,0:T(8,128)(2,1)S(1)} %collective-permute-done.3.refs_1_), channel_id=1, source_target_pairs={{0,8},{8,16},{16,24},{24,32},{32,40},{40,48},{48,56},{56,0},{64,72... | collective-permute-start | bytes 786440 | tf_op jit(solution)/shard_map/ppermute | solution.py:48
  26.7 26.0 %copy-start.12 = (bf16[8,128,128]{2,1,0:T(8,128)(2,1)}, bf16[8,128,128]{2,1,0:T(8,128)(2,1)S(1)}, u32[]{:S(2)}) copy-start(bf16[8,128,128]{2,1,0:T(8,128)(2,1)S(1)} %collective-permute-done.4.refs_2_) | copy-start | bytes 786436
  26.7 6.4 %collective-permute-start.6 = (bf16[8,128,128]{2,1,0:T(8,128)(2,1)S(1)}, bf16[8,128,128]{2,1,0:T(8,128)(2,1)S(1)}, u32[]{:S(2)}, u32[]{:S(2)}) collective-permute-start(bf16[8,128,128]{2,1,0:T(8,128)(2,1)S(1)} %collective-permute-done.4.refs_2_), channel_id=1, source_target_pairs={{0,56},{8,0},{16,8},{24,16},{32,24},{40,32},{48,40},{56,48},{64,12... | collective-permute-start | bytes 786440 | tf_op jit(solution)/shard_map/ppermute | solution.py:48
  33.1 14.4 %collective-permute-start.7 = (bf16[8,128,128]{2,1,0:T(8,128)(2,1)S(1)}, bf16[8,128,128]{2,1,0:T(8,128)(2,1)S(1)}, u32[]{:S(2)}, u32[]{:S(2)}) collective-permute-start(bf16[8,128,128]{2,1,0:T(8,128)(2,1)S(1)} %collective-permute-done.5.refs_3_), channel_id=1, source_target_pairs={{0,8},{8,16},{16,24},{24,32},{32,40},{40,48},{48,56},{56,0},{64,72... | collective-permute-start | bytes 786440 | tf_op jit(solution)/shard_map/ppermute | solution.py:48
  33.1 14.5 %collective-permute-start.8 = (bf16[8,128,128]{2,1,0:T(8,128)(2,1)S(1)}, bf16[8,128,128]{2,1,0:T(8,128)(2,1)S(1)}, u32[]{:S(2)}, u32[]{:S(2)}) collective-permute-start(bf16[8,128,128]{2,1,0:T(8,128)(2,1)S(1)} %collective-permute-done.6.refs_4_), channel_id=1, source_target_pairs={{0,56},{8,0},{16,8},{24,16},{32,24},{40,32},{48,40},{56,48},{64,12... | collective-permute-start | bytes 786440 | tf_op jit(solution)/shard_map/ppermute | solution.py:48
  47.5 5.1 %collective-permute-start.9 = (bf16[4,128,128]{2,1,0:T(8,128)(2,1)S(1)}, bf16[4,128,128]{2,1,0:T(8,128)(2,1)S(1)}, u32[]{:S(2)}, u32[]{:S(2)}) collective-permute-start(bf16[4,128,128]{2,1,0:T(8,128)(2,1)S(1)} %slice.52), channel_id=1, source_target_pairs={{0,8},{8,16},{16,24},{24,32},{32,40},{40,48},{48,56},{56,0},{64,72... | collective-permute-start | bytes 393224 | tf_op jit(solution)/shard_map/ppermute | solution.py:48
  47.7 5.0 %collective-permute-start.10 = (bf16[4,128,128]{2,1,0:T(8,128)(2,1)S(1)}, bf16[4,128,128]{2,1,0:T(8,128)(2,1)S(1)}, u32[]{:S(2)}, u32[]{:S(2)}) collective-permute-start(bf16[4,128,128]{2,1,0:T(8,128)(2,1)S(1)} %slice.53), channel_id=1, source_target_pairs={{0,56},{8,0},{16,8},{24,16},{32,24},{40,32},{48,40},{56,48},{64,12... | collective-permute-start | bytes 393224 | tf_op jit(solution)/shard_map/ppermute | solution.py:48
  62.6 51.1 %copy-start.37 = (bf16[256,172]{0,1:T(8,128)(2,1)S(1)}, bf16[256,172]{0,1:T(8,128)(2,1)}, u32[]{:S(2)}) copy-start(bf16[256,172]{0,1:T(8,128)(2,1)} %param.22) | copy-start | bytes 264196
  62.6 25.6 %all-to-all-start = ((f32[8,264,128]{2,1,0:T(8,128)}), f32[8,264,128]{2,1,0:T(8,128)S(1)}, u32[]{:S(2)}, u32[]{:S(2)}) async-start(f32[8,264,128]{2,1,0:T(8,128)} %bitcast.5), calls=%async_computation | async-start | bytes 2162688 | tf_op jit(solution)/shard_map/all_to_all | solution.py:305
  72.8 42.4 %copy-start.38 = (bf16[256,172]{0,1:T(8,128)(2,1)S(1)}, bf16[256,172]{0,1:T(8,128)(2,1)}, u32[]{:S(2)}) copy-start(bf16[256,172]{0,1:T(8,128)(2,1)} %param.21) | copy-start | bytes 264196
  72.8 129.8 %all-gather.2.cloned.1.call-start = ((), (), s32[]{:S(2)}) async-start(), calls=%async_computation.4 | async-start | bytes 2162688 | tf_op jit(solution)/shard_map/all_gather | solution.py:323
  88.4 41.1 %copy-start.42 = (f32[172]{0:T(256)S(1)}, f32[172]{0:T(256)}, u32[]{:S(2)}) copy-start(f32[172]{0:T(256)} %param.23) | copy-start | bytes 2068
  89.2 5.4 %collective-permute-start.11 = (bf16[2,256,128]{2,1,0:T(8,128)(2,1)S(1)}, bf16[2,256,128]{2,1,0:T(8,128)(2,1)S(1)}, u32[]{:S(2)}, u32[]{:S(2)}) collective-permute-start(bf16[2,256,128]{2,1,0:T(8,128)(2,1)S(1)} %get-tuple-element.15.hid), channel_id=1, source_target_pairs={{0,64},{64,128},{128,192},{192,0},{8,72},{72,136},{136,200},{200,8... | collective-permute-start | bytes 393224 | tf_op jit(solution)/shard_map/ppermute | solution.py:48
  89.5 5.1 %collective-permute-start.12 = (bf16[2,256,128]{2,1,0:T(8,128)(2,1)S(1)}, bf16[2,256,128]{2,1,0:T(8,128)(2,1)S(1)}, u32[]{:S(2)}, u32[]{:S(2)}) collective-permute-start(bf16[2,256,128]{2,1,0:T(8,128)(2,1)S(1)} %get-tuple-element.15.hid), channel_id=1, source_target_pairs={{0,192},{64,0},{128,64},{192,128},{8,200},{72,8},{136,72},{200,136... | collective-permute-start | bytes 393224 | tf_op jit(solution)/shard_map/ppermute | solution.py:48
  91.9 5.4 %collective-permute-start.13 = (bf16[2,256,128]{2,1,0:T(8,128)(2,1)S(1)}, bf16[2,256,128]{2,1,0:T(8,128)(2,1)S(1)}, u32[]{:S(2)}, u32[]{:S(2)}) collective-permute-start(bf16[2,256,128]{2,1,0:T(8,128)(2,1)S(1)} %get-tuple-element.15.hid), channel_id=1, source_target_pairs={{0,128},{64,192},{128,0},{192,64},{8,136},{72,200},{136,8},{200,72... | collective-permute-start | bytes 393224 | tf_op jit(solution)/shard_map/ppermute | solution.py:48
  97.4 45.7 %copy-start.30 = (s32[1,1,128]{2,1,0:T(1,128)S(1)}, s32[1,1,128]{2,1,0:T(1,128)}, u32[]{:S(2)}) copy-start(s32[1,1,128]{2,1,0:T(1,128)} %param.14) | copy-start | bytes 1540
  97.4 13.6 %collective-permute-start.14 = (bf16[8,256,128]{2,1,0:T(8,128)(2,1)S(1)}, bf16[8,256,128]{2,1,0:T(8,128)(2,1)S(1)}, u32[]{:S(2)}, u32[]{:S(2)}) collective-permute-start(bf16[8,256,128]{2,1,0:T(8,128)(2,1)S(1)} %constant_dynamic-update-slice_fusion.refs_0_), channel_id=1, source_target_pairs={{0,8},{8,16},{16,24},{24,32},{32,40},{40,48},{48,56},{56,0},{64,72... | collective-permute-start | bytes 1572872 | tf_op jit(solution)/shard_map/ppermute | solution.py:48
  97.7 13.4 %collective-permute-start.15 = (bf16[8,256,128]{2,1,0:T(8,128)(2,1)S(1)}, bf16[8,256,128]{2,1,0:T(8,128)(2,1)S(1)}, u32[]{:S(2)}, u32[]{:S(2)}) collective-permute-start(bf16[8,256,128]{2,1,0:T(8,128)(2,1)S(1)} %constant_dynamic-update-slice_fusion.refs_0_), channel_id=1, source_target_pairs={{0,56},{8,0},{16,8},{24,16},{32,24},{40,32},{48,40},{56,48},{64,12... | collective-permute-start | bytes 1572872 | tf_op jit(solution)/shard_map/ppermute | solution.py:48
  111.0 12.3 %collective-permute-start.16 = (bf16[8,256,128]{2,1,0:T(8,128)(2,1)S(1)}, bf16[8,256,128]{2,1,0:T(8,128)(2,1)S(1)}, u32[]{:S(2)}, u32[]{:S(2)}) collective-permute-start(bf16[8,256,128]{2,1,0:T(8,128)(2,1)S(1)} %collective-permute-done.14.refs_1_), channel_id=1, source_target_pairs={{0,8},{8,16},{16,24},{24,32},{32,40},{40,48},{48,56},{56,0},{64,72... | collective-permute-start | bytes 1572872 | tf_op jit(solution)/shard_map/ppermute | solution.py:48
  111.0 13.2 %collective-permute-start.17 = (bf16[8,256,128]{2,1,0:T(8,128)(2,1)S(1)}, bf16[8,256,128]{2,1,0:T(8,128)(2,1)}, u32[]{:S(2)}, u32[]{:S(2)}) collective-permute-start(bf16[8,256,128]{2,1,0:T(8,128)(2,1)S(1)} %collective-permute-done.15.refs_2_), channel_id=1, source_target_pairs={{0,56},{8,0},{16,8},{24,16},{32,24},{40,32},{48,40},{56,48},{64,12... | collective-permute-start | bytes 1572872 | tf_op jit(solution)/shard_map/ppermute | solution.py:48
  123.3 37.9 %copy-start.1 = (bf16[8,256,128]{2,1,0:T(8,128)(2,1)}, bf16[8,256,128]{2,1,0:T(8,128)(2,1)S(1)}, u32[]{:S(2)}) copy-start(bf16[8,256,128]{2,1,0:T(8,128)(2,1)S(1)} %collective-permute-done.16.refs_3_) | copy-start | bytes 1572868
  123.3 10.5 %collective-permute-start.18 = (bf16[8,256,128]{2,1,0:T(8,128)(2,1)S(1)}, bf16[8,256,128]{2,1,0:T(8,128)(2,1)S(1)}, u32[]{:S(2)}, u32[]{:S(2)}) collective-permute-start(bf16[8,256,128]{2,1,0:T(8,128)(2,1)S(1)} %collective-permute-done.16.refs_3_), channel_id=1, source_target_pairs={{0,8},{8,16},{16,24},{24,32},{32,40},{40,48},{48,56},{56,0},{64,72... | collective-permute-start | bytes 1572872 | tf_op jit(solution)/shard_map/ppermute | solution.py:48
  124.2 10.2 %collective-permute-start.19 = (bf16[8,256,128]{2,1,0:T(8,128)(2,1)}, bf16[8,256,128]{2,1,0:T(8,128)(2,1)S(1)}, u32[]{:S(2)}, u32[]{:S(2)}) collective-permute-start(bf16[8,256,128]{2,1,0:T(8,128)(2,1)} %collective-permute-done.17.refs_4_), channel_id=1, source_target_pairs={{0,56},{8,0},{16,8},{24,16},{32,24},{40,32},{48,40},{56,48},{64,12... | collective-permute-start | bytes 1572872 | tf_op jit(solution)/shard_map/ppermute | solution.py:48
  133.8 8.2 %collective-permute-start.20 = (bf16[4,256,128]{2,1,0:T(8,128)(2,1)S(1)}, bf16[4,256,128]{2,1,0:T(8,128)(2,1)S(1)}, u32[]{:S(2)}, u32[]{:S(2)}) collective-permute-start(bf16[4,256,128]{2,1,0:T(8,128)(2,1)S(1)} %slice.54), channel_id=1, source_target_pairs={{0,8},{8,16},{16,24},{24,32},{32,40},{40,48},{48,56},{56,0},{64,72... | collective-permute-start | bytes 786440 | tf_op jit(solution)/shard_map/ppermute | solution.py:48
  134.5 8.6 %collective-permute-start.21 = (bf16[4,256,128]{2,1,0:T(8,128)(2,1)S(1)}, bf16[4,256,128]{2,1,0:T(8,128)(2,1)S(1)}, u32[]{:S(2)}, u32[]{:S(2)}) collective-permute-start(bf16[4,256,128]{2,1,0:T(8,128)(2,1)S(1)} %slice.55), channel_id=1, source_target_pairs={{0,56},{8,0},{16,8},{24,16},{32,24},{40,32},{48,40},{56,48},{64,12... | collective-permute-start | bytes 786440 | tf_op jit(solution)/shard_map/ppermute | solution.py:48
  163.2 21.6 %all-to-all-start.1 = ((bf16[8,2,176,128]{3,2,1,0:T(8,128)(2,1)}), bf16[8,2,176,128]{3,2,1,0:T(8,128)(2,1)S(1)}, u32[]{:S(2)}, u32[]{:S(2)}) async-start(bf16[8,2,176,128]{3,2,1,0:T(8,128)(2,1)} %bitcast.44), calls=%async_computation.1 | async-start | bytes 1441792 | tf_op jit(solution)/shard_map/all_to_all | solution.py:339
  174.8 27.9 %copy-start.17 = (bf16[256,176]{1,0:T(8,128)(2,1)S(1)}, bf16[256,176]{1,0:T(8,128)(2,1)}, u32[]{:S(2)}) copy-start(bf16[256,176]{1,0:T(8,128)(2,1)} %get-tuple-element.50.neigh_second) | copy-start | bytes 270340
  (37 other events, 384.8 us)
Sparse Core Ops, SparseCore 0:
  89.3 73.1 all-gather.1
